TPU v7x, 32 devices: a whole 2x2x4 slice. The times are simulated.
32 devices in a mesh: row: 8 (over z, y), col: 4 (over x, core).
Axes of the slice: x: 2, y: 2, z: 4, core: 2. Of those that a mesh axis runs over, the one named last changes fastest.
Arguments:
- points: float32 [8192, 64], P(('col', 'row')), may hold values from -6 to 6
- feature_scale: float32 [64], replicated, may hold values from 0.1 to 0.5
- test_matrix: bfloat16 [8192, 256], P(('col', 'row')), may hold values from -6 to 6
- targets: float32 [8192], P(('col', 'row')), may hold values from -6 to 6
- ridge: float32 [1], replicated, may hold values from 0.5 to 2
Outputs:
- coefficients: float32 [8192], P(('col', 'row'))
- residual: float32 [8192], P(('col', 'row'))
- sketch: float32 [8192, 256], P(('col', 'row'))
All inputs are finite; a program needn't handle non-finite values.
Results may differ from a plain program's by a relative error of at most 0.012.
The roundings to bfloat16 on the way count: a program that leaves them out, or rounds other values in their place, can miss the bound.
Values may be sent and summed in bfloat16 or wider, within the bound.
A program may use at most 128 MiB of HBM per device.

v0:
```python
import jax
import jax.numpy as jnp
from jax import lax
from jax.sharding import PartitionSpec as P

ITERS = 2


def kernel_block(left, left_norm, right, right_norm):
    cross = lax.dot_general(
        left,
        right,
        (((1,), (1,)), ((), ())),
        precision=lax.Precision.HIGHEST,
        preferred_element_type=jnp.float32,
    )
    return jnp.exp(-0.5 * (left_norm[:, None] + right_norm[None, :] - 2.0 * cross))


def squared(scaled):
    return jnp.sum(scaled * scaled, axis=1)


def sketch_term(left, left_norm, right, right_norm, test_block):
    weights = kernel_block(left, left_norm, right, right_norm).astype(jnp.bfloat16)
    return jnp.dot(weights, test_block, preferred_element_type=jnp.float32)


def core_solve(lower, vector):
    middle = lax.linalg.triangular_solve(lower, vector[:, None], left_side=True, lower=True)
    return lax.linalg.triangular_solve(lower, middle, left_side=True, lower=True, transpose_a=True)[
        :, 0
    ]


def local(points, feature_scale, test_matrix, targets, ridge):
    ridge_value = ridge[0]
    scaled = points * feature_scale[None, :]
    test_wide = test_matrix.astype(jnp.float32)
    column_pts = lax.all_gather(scaled, "row", axis=0, tiled=True)
    column_rows = lax.all_gather(test_matrix, "row", axis=0, tiled=True)
    row_pts = lax.all_gather(scaled, "col", axis=0, tiled=True)
    row_norm = squared(row_pts)
    column_norm = squared(column_pts)
    sketch = lax.psum_scatter(
        sketch_term(row_pts, row_norm, column_pts, column_norm, column_rows),
        "col",
        scatter_dimension=0,
        tiled=True,
    )
    gram_test = lax.dot_general(
        test_wide,
        sketch,
        (((0,), (0,)), ((), ())),
        precision=lax.Precision.HIGHEST,
        preferred_element_type=jnp.float32,
    )
    gram_sketch = lax.dot_general(
        sketch,
        sketch,
        (((0,), (0,)), ((), ())),
        precision=lax.Precision.HIGHEST,
        preferred_element_type=jnp.float32,
    )
    total_test, total_sketch = lax.psum((gram_test, gram_sketch), ("row", "col"))
    core = ridge_value * total_test + total_sketch
    lower = jnp.linalg.cholesky(core)

    def operate(vector):
        column_vec = lax.all_gather(vector, "row", axis=0, tiled=True)
        weights = kernel_block(row_pts, row_norm, column_pts, column_norm)
        return (
            lax.psum_scatter(
                jnp.dot(
                    weights,
                    column_vec,
                    precision=lax.Precision.HIGHEST,
                    preferred_element_type=jnp.float32,
                ),
                "col",
                scatter_dimension=0,
                tiled=True,
            )
            + ridge_value * vector
        )

    def precondition(resid):
        local_proj = jnp.dot(
            resid, sketch, precision=lax.Precision.HIGHEST, preferred_element_type=jnp.float32
        )
        projected, square_sum = lax.psum((local_proj, jnp.sum(resid * resid)), ("row", "col"))
        solved = core_solve(lower, projected)
        precond = (
            resid
            - jnp.dot(
                sketch, solved, precision=lax.Precision.HIGHEST, preferred_element_type=jnp.float32
            )
        ) / ridge_value
        descent = (square_sum - jnp.sum(projected * solved)) / ridge_value
        return (precond, descent)

    coefficients = jnp.zeros_like(targets)
    resid = targets
    precond, descent = precondition(resid)
    direction = precond
    for turn in range(ITERS):
        image = operate(direction)
        step_size = descent / lax.psum(jnp.sum(direction * image), ("row", "col"))
        coefficients = coefficients + step_size * direction
        if turn + 1 < ITERS:
            resid = resid - step_size * image
            precond, fresh = precondition(resid)
            direction = precond + fresh / descent * direction
            descent = fresh
    residual = targets - operate(coefficients)
    return (coefficients, residual, sketch)


def solution(mesh):
    in_specs = (P(("col", "row"), None), P(), P(("col", "row"), None), P(("col", "row")), P())
    out_specs = (P(("col", "row")), P(("col", "row")), P(("col", "row"), None))
    return jax.shard_map(local, mesh=mesh, in_specs=in_specs, out_specs=out_specs, check_vma=False)
```

profile of v0, /device:TPU:0, one launch (start us, length us, event | category | flops | bytes accessed | tf_op | source)
XLA Modules:
  0.0 526.1 jit_solution(16225468923045808377)
XLA Ops:
  7.2 0.7 all-gather.5.cloned.1.call-update
  7.9 0.9 broadcast_multiply_fusion
  8.9 7.2 %all_gather.18 = f32[1024,64]{0,1:T(8,128)S(1)} all-gather(f32[256,64]{0,1:T(8,128)S(1)} %broadcast_multiply_fusion), channel_id=1, replica_groups=mesh['row'=8,'col'=4] {'col'}, dimensions={0}, use_global_device_ids=true | all-gather | bytes 327680 | tf_op jit(solution)/shard_map/all_gather | solution.py:42
  16.1 32.4 %all_gather.19 = f32[2048,64]{0,1:T(8,128)S(1)} all-gather(f32[256,64]{0,1:T(8,128)S(1)} %broadcast_multiply_fusion), channel_id=1, replica_groups=mesh['row'=8,'col'=4] {'row'}, dimensions={0}, use_global_device_ids=true | all-gather | bytes 589824 | tf_op jit(solution)/shard_map/all_gather | solution.py:40
  48.5 0.1 multiply_reduce_fusion
  48.6 10.2 %multiply_exponential_fusion = f32[1024,2048]{1,0:T(8,128)} fusion(f32[1024,64]{0,1:T(8,128)S(1)} %all_gather.18, f32[2048,64]{0,1:T(8,128)S(1)} %all_gather.19, f32[2048]{0:T(1024)S(1)} %multiply_reduce_fusion, f32[1024]{0:T(1024)S(1)} %multiply_reduce_fusion.1), kind=kOutput, calls=%fused_computation.2 | convolution fusion | flops 1619001344 | bytes 9187328 | tf_op jit(solution)/shard_map/dot_general | solution.py:10
  58.8 5.9 %fusion = f32[1024,256]{1,0:T(8,128)} fusion(bf16[2048,256]{1,0:T(8,128)(2,1)} %all-gather.5.cloned.1.call-done, f32[1024,2048]{1,0:T(8,128)} %multiply_exponential_fusion), kind=kOutput, calls=%fused_computation.3 | convolution fusion | flops 1075838976 | bytes 10485760 | tf_op jit(solution)/shard_map/dot_general | solution.py:26
  64.8 25.8 %reduce-scatter.2.cloned.1.call-done = f32[256,256]{1,0:T(8,128)} async-done(((f32[1024,256]{1,0:T(8,128)}), f32[256,256]{1,0:T(8,128)}) %reduce-scatter.2.cloned.1.call-update) | async-done | bytes 262160 | tf_op jit(solution)/shard_map/reduce_scatter | solution.py:45
  90.7 2.1 convolution_bitcast_fusion
  92.8 2.4 fusion.23
  95.9 0.6 dynamic-slice.10
  97.1 1.2 fusion.22
  98.3 39.6 %psum.57 = f32[256]{0:T(256)S(1)} all-reduce(f32[256]{0:T(256)S(1)} %bitcast.193), channel_id=1, replica_groups=mesh['row'=8,'col'=4] {'row','col'}, use_global_device_ids=true, to_apply=%region_5.6 | all-reduce | flops 256 | bytes 2048 | tf_op jit(solution)/shard_map/psum | solution.py:91
  137.8 87.4 %all-reduce.9.cloned.1.call-done = (f32[256,256]{0,1:T(8,128)}, f32[256,256]{0,1:T(8,128)}) async-done(((f32[256,256]{0,1:T(8,128)}, f32[256,256]{0,1:T(8,128)}), (f32[256,256]{0,1:T(8,128)}, f32[256,256]{0,1:T(8,128)})) %all-reduce.9.cloned.1.call-update) | async-done | bytes 524304 | tf_op jit(solution)/shard_map/psum | solution.py:65
  225.3 1.1 multiply_add_fusion
  226.3 0.1 copy.11
  226.5 11.7 %cholesky.50 = f32[128,128]{1,0:T(8,128)S(1)} custom-call(f32[128,128]{1,0:T(8,128)S(1)} %cholesky.118), custom_call_target="Cholesky" | custom-call | tf_op jit(solution)/shard_map/jit(cholesky)/cholesky | solution.py:67
  238.3 9.8 %custom-call.17 = f32[1,128,128]{1,2,0:T(8,128)S(1)} custom-call(f32[1,128,128]{2,1,0:T(8,128)S(1)} %get-tuple-element.58), custom_call_target="InvertDiagBlocksLowerTriangular" | custom-call | tf_op jit(solution)/shard_map/jit(cholesky)/cholesky | solution.py:67
  248.1 0.2 constant_dynamic-update-slice_fusion.1
  248.3 0.3 convolution_subtract_fusion
  248.6 11.7 %cholesky.105 = f32[128,128]{1,0:T(8,128)S(1)} custom-call(f32[128,128]{1,0:T(8,128)S(1)} %convolution_subtract_fusion), custom_call_target="Cholesky" | custom-call | tf_op jit(solution)/shard_map/jit(cholesky)/cholesky | solution.py:67
  260.3 0.6 compare_reduce_fusion
  262.2 0.1 broadcast.158
  262.3 3.8 while.8
  262.3 0.6 fusion.60
  262.9 1.3 bitcast_dynamic-update-slice_fusion.2
  264.3 0.6 fusion.60
  264.8 1.3 bitcast_dynamic-update-slice_fusion.2
  266.2 19.9 %custom-call.21 = f32[2,128,128]{1,2,0:T(8,128)S(1)} custom-call(f32[2,128,128]{2,1,0:T(8,128)S(1)} %get-tuple-element.34), custom_call_target="InvertDiagBlocksLowerTriangular" | custom-call | tf_op jit(solution)/shard_map/triangular_solve/custom-call.4 | solution.py:31
  286.1 0.2 convolution_bitcast_fusion.12
  286.2 0.2 fusion.5
  286.4 0.2 convolution_bitcast_fusion.10
  286.6 0.2 convolution_bitcast_fusion.9
  286.8 0.2 fusion.4
  287.0 0.2 convolution_bitcast_fusion.7
  287.2 0.6 multiply_reduce_fusion.5
  287.8 1.2 fusion.20
  289.0 0.7 multiply_reduce_fusion.6
  289.7 19.4 %all-gather = f32[8,1,256]{2,1,0:T(1,128)S(1)} all-gather(f32[1,1,256]{2,1,0:T(1,128)S(1)} %bitcast.177), channel_id=1, replica_groups=mesh['row'=8,'col'=4] {'row'}, dimensions={0}, use_global_device_ids=true | all-gather | bytes 9216 | tf_op jit(solution)/shard_map/all_gather | solution.py:70
  309.1 9.4 %fusion.24 = f32[1,1024]{1,0:T(1,128)S(1)} fusion(f32[1024,2048]{1,0:T(8,128)} %multiply_exponential_fusion, f32[2048,1]{0,1:T(1,128)S(1)} %bitcast.179), kind=kOutput, calls=%fused_computation.74 | convolution fusion | flops 25165824 | bytes 8400896 | tf_op jit(solution)/shard_map/dot_general | solution.py:74
  318.5 5.7 %all-reduce.1 = f32[1024]{0:T(1024)S(1)} all-reduce(f32[1024]{0:T(1024)S(1)} %bitcast.182), channel_id=3, replica_groups=mesh['row'=8,'col'=4] {'col'}, use_global_device_ids=true, to_apply=%region_13.16.clone | all-reduce | flops 1024 | bytes 8192
  324.1 0.7 multiply_reduce_fusion.4
  324.8 37.1 %all-reduce.5 = (f32[]{:T(128)}, f32[]{:T(128)}) all-reduce(f32[]{:T(128)} %get-tuple-element.59, f32[]{:T(128)} %multiply_reduce_fusion.4), channel_id=1, replica_groups=mesh['row'=8,'col'=4] {'row','col'}, use_global_device_ids=true, to_apply=%region_1.0 | all-reduce | flops 2 | bytes 16 | tf_op jit(solution)/shard_map/psum | solution.py:91
  363.8 0.7 multiply_reduce_fusion.3
  364.5 0.2 fusion.25
  364.7 41.9 %all-reduce.4 = (f32[256]{0:T(256)S(1)}, f32[]{:T(128)}) all-reduce(f32[256]{0:T(256)S(1)} %bitcast.197, f32[]{:T(128)} %get-tuple-element.51), channel_id=1, replica_groups=mesh['row'=8,'col'=4] {'row','col'}, use_global_device_ids=true, to_apply=%region_18.21 | all-reduce | flops 257 | bytes 2056 | tf_op jit(solution)/shard_map/psum | solution.py:91
  406.7 0.2 convolution_bitcast_fusion.6
  406.8 0.2 fusion.3
  407.0 0.2 convolution_bitcast_fusion.4
  407.2 0.2 convolution_bitcast_fusion.3
  407.4 0.2 fusion.2
  407.6 0.2 convolution_bitcast_fusion.1
  407.8 0.7 multiply_reduce_fusion.2
  409.8 0.3 fusion.19
  410.1 0.1 divide_add_fusion
  410.1 19.7 %all-gather.1 = f32[8,1,256]{2,1,0:T(1,128)S(1)} all-gather(f32[1,1,256]{2,1,0:T(1,128)S(1)} %bitcast.185), channel_id=1, replica_groups=mesh['row'=8,'col'=4] {'row'}, dimensions={0}, use_global_device_ids=true | all-gather | bytes 9216 | tf_op jit(solution)/shard_map/all_gather | solution.py:70
  429.8 9.4 %fusion.26 = f32[1,1024]{1,0:T(1,128)S(1)} fusion(f32[1024,2048]{1,0:T(8,128)} %multiply_exponential_fusion, f32[2048,1]{0,1:T(1,128)S(1)} %bitcast.180), kind=kOutput, calls=%fused_computation.76 | convolution fusion | flops 25165824 | bytes 8400896 | tf_op jit(solution)/shard_map/dot_general | solution.py:74
  439.2 5.7 %all-reduce.2 = f32[1024]{0:T(1024)S(1)} all-reduce(f32[1024]{0:T(1024)S(1)} %bitcast.183), channel_id=4, replica_groups=mesh['row'=8,'col'=4] {'col'}, use_global_device_ids=true, to_apply=%region_20.23.clone | all-reduce | flops 1024 | bytes 8192
  444.9 0.7 fusion.16
  445.6 37.1 %psum.63 = f32[]{:T(128)} all-reduce(f32[]{:T(128)} %fusion.16), channel_id=1, replica_groups=mesh['row'=8,'col'=4] {'row','col'}, use_global_device_ids=true, to_apply=%region_22.25 | all-reduce | flops 1 | bytes 8 | tf_op jit(solution)/shard_map/psum | solution.py:108
  483.4 20.4 %all-gather.2 = f32[8,1,256]{2,1,0:T(1,128)S(1)} all-gather(f32[1,1,256]{2,1,0:T(1,128)S(1)} %bitcast.189), channel_id=1, replica_groups=mesh['row'=8,'col'=4] {'row'}, dimensions={0}, use_global_device_ids=true | all-gather | bytes 9216 | tf_op jit(solution)/shard_map/all_gather | solution.py:70
  503.9 9.4 %fusion.27 = f32[1,1024]{1,0:T(1,128)S(1)} fusion(f32[1024,2048]{1,0:T(8,128)} %multiply_exponential_fusion, f32[2048,1]{0,1:T(1,128)S(1)} %bitcast.178), kind=kOutput, calls=%fused_computation.77 | convolution fusion | flops 25165824 | bytes 8400896 | tf_op jit(solution)/shard_map/dot_general | solution.py:74
  513.3 5.7 %all-reduce.3 = f32[1024]{0:T(1024)S(1)} all-reduce(f32[1024]{0:T(1024)S(1)} %bitcast.181), channel_id=5, replica_groups=mesh['row'=8,'col'=4] {'col'}, use_global_device_ids=true, to_apply=%region_23.26.clone | all-reduce | flops 1024 | bytes 8192
  518.9 0.6 fusion.14
  (30 shorter events, 0.4 us)
Async XLA Ops:
  7.2 51.7 %all-gather.5.cloned.1.call-start = ((), (), s32[]{:S(2)}) async-start(), calls=%async_computation.1 | async-start | bytes 1179648 | tf_op jit(solution)/shard_map/all_gather | solution.py:41
  7.9 82.8 %reduce-scatter.2.cloned.1.call-start = ((), (), s32[]{:S(2)}) async-start(), calls=%async_computation.2 | async-start | bytes 1310720 | tf_op jit(solution)/shard_map/reduce_scatter | solution.py:45
  58.8 31.8 %copy-start.1 = (bf16[256,256]{1,0:T(8,128)(2,1)S(1)}, bf16[256,256]{1,0:T(8,128)(2,1)}, u32[]{:S(2)}) copy-start(bf16[256,256]{1,0:T(8,128)(2,1)} %param.11) | copy-start | bytes 393220
  58.8 37.1 %copy-start.4 = (u32[32]{0:T(128)S(1)}, u32[32]{0:T(128)}, u32[]{:S(2)}) copy-start(u32[32]{0:T(128)} %constant.130) | copy-start | bytes 388
  58.8 38.3 %copy-start.2 = (f32[256]{0:T(256)S(1)}, f32[256]{0:T(256)}, u32[]{:S(2)}) copy-start(f32[256]{0:T(256)} %param.12) | copy-start | bytes 3076
  64.8 160.5 %all-reduce.9.cloned.1.call-start = ((), (), s32[]{:S(2)}) async-start(), calls=%async_computation.3 | async-start | bytes 1048576 | tf_op jit(solution)/shard_map/psum | solution.py:65
  90.7 273.9 %copy-start = (f32[256,256]{1,0:T(8,128)S(1)}, f32[256,256]{1,0:T(8,128)}, u32[]{:S(2)}) copy-start(f32[256,256]{1,0:T(8,128)} %reduce-scatter.2.cloned.1.call-done) | copy-start | bytes 786436
  483.4 36.1 %copy-start.3 = (f32[256]{0:T(256)}, f32[256]{0:T(256)S(1)}, u32[]{:S(2)}) copy-start(f32[256]{0:T(256)S(1)} %multiply_add_fusion.1) | copy-start | bytes 3076
Sparse Core Ops, SparseCore 0:
  10.1 45.6 all-gather.4
  64.9 25.7 reduce-scatter.1
  97.0 128.2 all-reduce.8
where the time goes:
time: 527 us; the launch traced here: 526 us
  blocking collectives  272 us (52%)
  waiting for transfers between devices  114 us (22%)
  other arithmetic  60.7 us (12%)
  matrix products  54.4 us (10%)
  between operations  20.4 us (4%)
    psum x3, blocking collectives, precondition(): lax.psum((local_proj, jnp.sum(resid * resid)), ('row', 'col'))  119 us
    psum x1, waiting for transfers between devices, local(): lax.psum((gram_test, gram_sketch), ('row', 'col'))  87.4 us
    all_gather x3, blocking collectives, operate(): column_vec = lax.all_gather(vector, 'row', axis=0, tiled=True)  59.5 us
    psum x1, blocking collectives, local(): step_size = descent / lax.psum(jnp.sum(direction * image), ('row', 'col'))  37.1 us
    another operation x6, other arithmetic, local(): lower = jnp.linalg.cholesky(core)  33.9 us
    all_gather x1, blocking collectives, local(): column_pts = lax.all_gather(scaled, 'row', axis=0, tiled=True)  32.4 us
    dot_general x3, matrix products, operate(): jnp.dot(weights, column_vec, precision=lax.Precision.HIGHEST, preferred_e...  28.2 us
    reduce_scatter x1, waiting for transfers between devices, local(): lax.psum_scatter(sketch_term(row_pts, row_norm, column_pts, column_norm,...  25.8 us
  transfers between devices with their start and end apart: 3, of which 2 were waited for; matrix products, arithmetic and copies ran while one was open for 2% of the time, Pallas kernels for 0%

commit v1 on v0

v1 whole, which is shorter than its diff:
```python
import functools

import jax
import jax.numpy as jnp
from jax import lax
from jax.experimental import pallas as pl
from jax.experimental.pallas import tpu as pltpu
from jax.sharding import PartitionSpec as P

MESH = pl.DeviceIdType.MESH
EXACT = lax.Precision.HIGHEST
NN = (((1,), (0,)), ((), ()))
NT = (((1,), (1,)), ((), ()))
TN = (((0,), (0,)), ((), ()))
X_COL, PAIR, SKETCH, CORE, CORE_ROW, CORE_ALL, CORE_COL, W_ROW, W_COL = range(9)
Z_ROW, Q_COL, A_ROW, A_COL = (9, 13), (10, 14), (11, 15), (12, 16)
ROUNDS = 17
CORES = 2


def exact(left, right, dims):
    return lax.dot_general(
        left, right, dims, precision=EXACT, preferred_element_type=jnp.float32
    )


def invert(a):
    size, width = a.shape[0], 4
    lane = lax.broadcasted_iota(jnp.int32, a.shape, 1)
    lane_row = lane[0:1, :]

    def pivots(a, k):
        entry = [
            [jnp.broadcast_to(a[k + i : k + i + 1, k + j : k + j + 1], (1, size)) for j in range(width)]
            for i in range(width)
        ]
        rows = [a[k + i : k + i + 1, :] for i in range(width)]
        cols = [a[:, k + i : k + i + 1] for i in range(width)]
        for t in range(width):
            inverse = 1.0 / entry[t][t]
            here = lane_row == k + t
            rows[t] = jnp.where(here, inverse, rows[t] * inverse)
            for j in range(t + 1, width):
                entry[t][j] = entry[t][j] * inverse
            for i in range(width):
                if i != t:
                    factor = entry[i][t]
                    rows[i] = jnp.where(here, 0.0, rows[i]) - factor * rows[t]
                    for j in range(t + 1, width):
                        entry[i][j] = entry[i][j] - factor * entry[t][j]
        out = jnp.where((lane >= k) & (lane < k + width), 0.0, a)
        for t in range(width):
            out = out - cols[t] * rows[t]
        return out, rows

    def turn(_, a):
        a, upper = pivots(a, 0)
        a = jnp.concatenate(upper + [a[width:, :]], axis=0)
        a, lower = pivots(a, width)
        a = jnp.concatenate([a[8:, :], a[:width, :]] + lower, axis=0)
        return pltpu.roll(a, size - 8, 1)

    return lax.fori_loop(0, size // 8, turn, a)


def kernel(
    R, C, pts, scale, test, tgt, ridge, coef_out, resid_out, sketch_out,
    xrow, trow, xcol, left, left_norm, kmat, part, pair, srecv, core, crecv, crow, cgath, call, inv,
    vrow, vcol, qpart, qcol, send, recv, gather_send, gather_recv,
):
    r, c = lax.axis_index("row"), lax.axis_index("col")
    n, feats = pts.shape
    rank = test.shape[1]
    chunk = rank // C
    piece = chunk // R
    B = R // 4 if R % 4 == 0 else 1
    A = R // B
    half = rank // 2
    lam = ridge[0, 0]

    def to_row(i):
        return (lax.rem(r + i, R), c)

    def to_col(i):
        return (r, lax.rem(c + i, C))

    def copy(src, dst, out, into, dev):
        return pltpu.make_async_remote_copy(
            src_ref=src, dst_ref=dst, send_sem=out, recv_sem=into,
            device_id=dev, device_id_type=MESH,
        )

    def push(src, dst, k, dev):
        copy(src, dst, send.at[k], recv.at[k], dev).start()

    def spread_row(buf, k):
        for i in range(1, R):
            push(buf.at[r], buf.at[r], k, to_row(i))

    def spread_col(buf, k):
        for i in range(1, C):
            push(buf.at[c], buf.at[c], k, to_col(i))

    def arrived(buf, k):
        part_of = buf.at[pl.ds(0, buf.shape[0] - 1)]
        pltpu.make_async_copy(part_of, part_of, recv.at[k]).wait()

    def sent(buf, k):
        part_of = buf.at[pl.ds(0, buf.shape[0] - 1)]
        pltpu.make_async_copy(part_of, part_of, send.at[k]).wait()

    def total(buf):
        acc = buf[0]
        for i in range(1, buf.shape[0]):
            acc = acc + buf[i]
        return acc

    barrier = pltpu.get_barrier_semaphore()
    for i in range(1, R):
        pl.semaphore_signal(barrier, inc=1, device_id=to_row(i), device_id_type=MESH)
    for i in range(1, C):
        pl.semaphore_signal(barrier, inc=1, device_id=to_col(i), device_id_type=MESH)

    scaled = pts[...] * scale[...]
    high = scaled.astype(jnp.bfloat16).astype(jnp.float32)
    both = jnp.concatenate([high, scaled - high], axis=1).astype(jnp.bfloat16)
    xrow[r] = both
    xcol[c] = both
    trow[r] = test[...]
    pl.semaphore_wait(barrier, R + C - 2)
    spread_col(xcol, X_COL)

    along, across = lax.div(r, B), lax.rem(r, B)
    stores = (xrow, trow)

    def hops(slot, s):
        origin = lax.div(slot, B)

        def make(kind, dev):
            return copy(
                stores[s].at[slot], stores[s].at[slot], gather_send.at[s, slot, kind],
                gather_recv.at[s, slot], (dev, c),
            )

        out = [
            ((origin <= along) & (along + 1 < A), make(0, lax.rem(r + B, R))),
            ((origin >= along) & (along >= 1), make(1, lax.rem(r + R - B, R))),
        ]
        for i in range(1, B):
            out.append((None, make(1 + i, along * B + lax.rem(across + i, B))))
        return out

    def forward(slot, s):
        for condition, move in hops(slot, s):
            if condition is None:
                move.start()
            else:
                pl.when(condition)(move.start)

    def landed(slot, s):
        here = stores[s].at[slot]
        pltpu.make_async_copy(here, here, gather_recv.at[s, slot]).wait()

    ones = jnp.ones((8, 128), jnp.float32)

    def pair_sum(x):
        swapped = pltpu.roll(x, feats, 1)
        return swapped, x * (x + swapped)

    def consume(slot, first=False):
        y = xrow[slot]
        right_norm = -0.5 * exact(ones, pair_sum(y.astype(jnp.float32))[1], NT)[0:1, :]
        right = jnp.concatenate([y, y], axis=1)

        def block(m, carry):
            cross = lax.dot_general(left[m], right, NT, preferred_element_type=jnp.float32)
            norm = left_norm[m]
            weights = jnp.exp(cross + jnp.concatenate([norm] * (n // 128), axis=1) + right_norm)
            kmat[slot, m] = weights
            term = lax.dot_general(
                weights.astype(jnp.bfloat16), trow[slot], NN, preferred_element_type=jnp.float32
            )
            part[m] = term if first else part[m] + term
            return carry

        lax.fori_loop(0, C, block, 0)

    def line(d):
        return ((along >= d, r - d * B), (along + d < A, r + d * B))

    for s in range(2):
        forward(r, s)
    arrived(xcol, X_COL)
    for m in range(C):
        x = xcol[m]
        swapped, square = pair_sum(x.astype(jnp.float32))
        left[m] = jnp.concatenate([x, swapped.astype(jnp.bfloat16)], axis=1)
        left_norm[m] = jnp.broadcast_to(-0.5 * jnp.sum(square, axis=1, keepdims=True), (n, 128))
    consume(r, first=True)
    for d in range(1, A):
        for s in range(2):
            for there, slot in line(d):

                @pl.when(there)
                def _(slot=slot, s=s):
                    landed(slot, s)
                    forward(slot, s)

        for there, slot in line(d):
            pl.when(there)(functools.partial(consume, slot))
    for i in range(1, B):
        other = along * B + lax.rem(across + i, B)
        for d in range(A):
            for there, slot in line(d) if d else ((None, r),):
                slot = slot - r + other

                def use(slot=slot):
                    landed(slot, 0)
                    landed(slot, 1)
                    consume(slot)

                if there is None:
                    use()
                else:
                    pl.when(there)(use)

    chip, side = lax.div(c, CORES), lax.rem(c, CORES)
    chips = C // CORES
    for i in range(chips):
        m = lax.rem(chip + 1 + i, chips) * CORES + 1 - side
        push(part.at[m], pair.at[m - 1 + side], PAIR, (r, chip * CORES + 1 - side))
    mine = pair.at[pl.ds(0, chips)]
    pltpu.make_async_copy(mine, mine, recv.at[PAIR]).wait()
    for i in range(chips):
        m = lax.rem(chip + 1 + i, chips)
        summed = part[m * CORES + side] + pair[m * CORES]
        if i < chips - 1:
            part[m * CORES + side] = summed
            push(part.at[m * CORES + side], srecv.at[chip], SKETCH, (r, m * CORES + side))
        else:
            srecv[chip] = summed
    arrived(srecv, SKETCH)
    sketch = total(srecv)
    sketch_out[...] = sketch

    resid = jnp.broadcast_to(tgt[...], (8, n))
    local = exact(lam * test[...].astype(jnp.float32) + sketch, sketch, TN)
    for i in range(C):
        core[i] = local[i * chunk : (i + 1) * chunk, :]
    for i in range(1, C):
        push(core.at[lax.rem(c + i, C)], crecv.at[c], CORE, to_col(i))
    w_row, w_col = vrow.at[0], vcol.at[0]
    w_row[r, :, 0:rank] = exact(resid, sketch, NN)[0:1, :]
    w_row[r, :, rank : rank + 128] = jnp.zeros((1, 128), jnp.float32)
    spread_row(w_row, W_ROW)
    crecv[c] = core[c]
    arrived(crecv, CORE)
    summed = total(crecv)
    for i in range(R):
        crow[0, i] = summed[i * piece : (i + 1) * piece, :]
    for i in range(1, R):
        push(crow.at[0, lax.rem(r + i, R)], crow.at[1, r], CORE_ROW, to_row(i))
    arrived(w_row, W_ROW)
    w_col[c] = total(w_row)
    spread_col(w_col, W_COL)
    crow[1, r] = crow[0, r]
    arrived(crow.at[1], CORE_ROW)
    cgath[r] = total(crow.at[1])
    spread_row(cgath, CORE_ALL)
    arrived(cgath, CORE_ALL)
    call[c] = cgath[...].reshape(chunk, rank)
    spread_col(call, CORE_COL)
    arrived(w_col, W_COL)
    w = total(w_col)[:, 0:rank]
    arrived(call, CORE_COL)

    whole = call[...].reshape(rank, rank)
    top, up = whole[:half, :half], whole[:half, half:]
    down, low = whole[half:, :half], whole[half:, half:]
    first = invert(top)
    above = exact(first, up, NN)
    below = exact(down, first, NN)
    second = invert(low - exact(down, above, NN))
    corner = exact(second, below, NN)
    inv[:half, :half] = first + exact(above, corner, NN)
    inv[:half, half:] = -exact(above, second, NN)
    inv[half:, :half] = -corner
    inv[half:, half:] = second

    def lanes(x):
        return jnp.sum(x, axis=1, keepdims=True)

    def wide(x):
        return jnp.broadcast_to(x[0:1, :], (1, 128))

    def precondition(resid, w):
        solved = exact(jnp.broadcast_to(w, (8, rank)), inv[...], NN)
        return (resid - exact(solved, sketch_out[...], NT)) / lam

    def operate(vector, inner, k):
        vec, sums = vrow.at[1 + 2 * k], qcol.at[k]
        vec[r, :, 0:n] = vector[0:1, :]
        vec[r, :, n : n + 128] = wide(lanes(inner))
        spread_row(vec, Z_ROW[k])
        arrived(vec, Z_ROW[k])
        inner_sum = total(vec)[:, n : n + 128]
        pieces = [vec[j] for j in range(R)]

        def block(i, carry):
            m = lax.rem(c + i, C)
            acc = jnp.zeros((n, 128), jnp.float32)
            for j in range(R):
                for h in range(0, n, 128):
                    acc += kmat[j, m, :, h : h + 128] * pieces[j][:, h : h + 128]
            qpart[k, m, :, 0:n] = exact(ones, acc, NT)[0:1, :]
            qpart[k, m, :, n : n + 128] = inner_sum

            @pl.when(i < C)
            def _():
                push(qpart.at[k, m], sums.at[c], Q_COL[k], (r, m))

            return carry

        lax.fori_loop(1, C + 1, block, 0)
        sums[c] = qpart[k, c]
        arrived(sums, Q_COL[k])
        out = total(sums)
        return out[:, 0:n] + lam * vector, out[:, n : n + 1]

    def reduce_all(row, scalar, k):
        across, along = vrow.at[2 + 2 * k], vcol.at[1 + k]
        across[r, :, 0:rank] = row[0:1, :]
        across[r, :, rank : rank + 128] = wide(scalar)
        spread_row(across, A_ROW[k])
        arrived(across, A_ROW[k])
        along[c] = total(across)
        spread_col(along, A_COL[k])
        arrived(along, A_COL[k])
        out = total(along)
        return out[:, 0:rank], out[:, rank : rank + 1]

    direction = precondition(resid, w)
    image, descent = operate(direction, resid * direction, 0)
    projected, curve = reduce_all(exact(image, sketch_out[...], NN), lanes(direction * image), 0)
    step = descent / curve
    coef = step * direction
    resid = resid - step * image
    precond = precondition(resid, w - step * projected)
    next_image, fresh = operate(precond, resid * precond, 1)
    ratio = fresh / descent
    direction = precond + ratio * direction
    image = next_image + ratio * image
    _, curve = reduce_all(direction, lanes(direction * image), 1)
    step = fresh / curve
    coef_out[...] = (coef + step * direction)[0:1, :]
    resid_out[...] = (resid - step * image)[0:1, :]

    for s in range(2):
        for d in range(A):
            for there, slot in line(d) if d else ((None, r),):
                for condition, move in hops(slot, s):
                    both = [x for x in (there, condition) if x is not None]
                    if both:
                        pl.when(functools.reduce(jnp.logical_and, both))(move.wait_send)
                    else:
                        move.wait_send()
    sent(xcol, X_COL)
    pltpu.make_async_copy(mine, mine, send.at[PAIR]).wait()
    sent(srecv, SKETCH)
    sent(crecv, CORE)
    sent(crow.at[1], CORE_ROW)
    sent(cgath, CORE_ALL)
    sent(call, CORE_COL)
    sent(w_row, W_ROW)
    sent(w_col, W_COL)
    for k in range(2):
        sent(vrow.at[1 + 2 * k], Z_ROW[k])
        sent(qcol.at[k], Q_COL[k])
        sent(vrow.at[2 + 2 * k], A_ROW[k])
        sent(vcol.at[1 + k], A_COL[k])


def local(R, C, points, feature_scale, test_matrix, targets, ridge):
    n, feats = points.shape
    rank = test_matrix.shape[1]
    f32, half = jnp.float32, jnp.bfloat16
    vmem = pl.BlockSpec(memory_space=pltpu.VMEM)
    coef, resid, sketch = pl.pallas_call(
        functools.partial(kernel, R, C),
        out_shape=(
            jax.ShapeDtypeStruct((1, n), f32),
            jax.ShapeDtypeStruct((1, n), f32),
            jax.ShapeDtypeStruct((n, rank), f32),
        ),
        in_specs=[vmem, vmem, vmem, vmem, pl.BlockSpec(memory_space=pltpu.SMEM)],
        out_specs=(vmem, vmem, vmem),
        scratch_shapes=[
            pltpu.VMEM((R, n, 2 * feats), half),
            pltpu.VMEM((R, n, rank), half),
            pltpu.VMEM((C, n, 2 * feats), half),
            pltpu.VMEM((C, n, 4 * feats), half),
            pltpu.VMEM((C, n, 128), f32),
            pltpu.VMEM((R, C, n, n), f32),
            pltpu.VMEM((C, n, rank), f32),
            pltpu.VMEM((C, n, rank), f32),
            pltpu.VMEM((C // CORES, n, rank), f32),
            pltpu.VMEM((C, rank // C, rank), f32),
            pltpu.VMEM((C, rank // C, rank), f32),
            pltpu.VMEM((2, R, rank // C // R, rank), f32),
            pltpu.VMEM((R, rank // C // R, rank), f32),
            pltpu.VMEM((C, rank // C, rank), f32),
            pltpu.VMEM((rank, rank), f32),
            pltpu.VMEM((5, R, 1, n + 128), f32),
            pltpu.VMEM((3, C, 1, n + 128), f32),
            pltpu.VMEM((2, C, 1, n + 128), f32),
            pltpu.VMEM((2, C, 1, n + 128), f32),
            pltpu.SemaphoreType.DMA((ROUNDS,)),
            pltpu.SemaphoreType.DMA((ROUNDS,)),
            pltpu.SemaphoreType.DMA((2, R, 6)),
            pltpu.SemaphoreType.DMA((2, R)),
        ],
        compiler_params=pltpu.CompilerParams(
            collective_id=0, has_side_effects=True, vmem_limit_bytes=56 * 1024 * 1024
        ),
    )(points, feature_scale.reshape(1, feats), test_matrix, targets.reshape(1, n), ridge.reshape(1, 1))
    return coef.reshape(n), resid.reshape(n), sketch


def solution(mesh):
    R, C = mesh.shape["row"], mesh.shape["col"]
    in_specs = (P(("col", "row"), None), P(), P(("col", "row"), None), P(("col", "row")), P())
    out_specs = (P(("col", "row")), P(("col", "row")), P(("col", "row"), None))
    return jax.shard_map(
        functools.partial(local, R, C), mesh=mesh, in_specs=in_specs, out_specs=out_specs,
        check_vma=False,
    )
```

time: 527 us -> 109 us (0.21)
  blocking collectives: 272 us -> 0 us
  waiting for transfers between devices: 114 us -> 0 us
  Pallas kernels: 0 us -> 102 us
  other arithmetic: 60.7 us -> 0 us
  matrix products: 54.4 us -> 0 us
  between operations: 20.4 us -> 1.3 us
    psum x4 -> x0, blocking collectives: 156 us -> none  [the longest x3 119 us: precondition(): lax.psum((local_proj, jnp.sum(resid * resid)), ('row', 'col'))]
    pallas_call x0 -> x1, Pallas kernels: none -> 102 us  [local(): pl.pallas_call(functools.partial(kernel, R, C), out_shape=(jax.ShapeDtype...]
    all_gather x5 -> x0, blocking collectives: 99.1 us -> none  [the longest x3 59.5 us: operate(): column_vec = lax.all_gather(vector, 'row', axis=0, tiled=True)]
    psum x1 -> x0, waiting for transfers between devices: 87.4 us -> none  [local(): lax.psum((gram_test, gram_sketch), ('row', 'col'))]
    another operation x12 -> x0, other arithmetic: 53.9 us -> none  [the longest x6 33.9 us: local(): lower = jnp.linalg.cholesky(core)]
    dot_general x11 -> x0, matrix products: 51.7 us -> none  [the longest x3 28.2 us: operate(): jnp.dot(weights, column_vec, precision=lax.Precision.HIGHEST, preferred_e...]
    reduce_scatter x1 -> x0, waiting for transfers between devices: 25.8 us -> none  [local(): lax.psum_scatter(sketch_term(row_pts, row_norm, column_pts, column_norm,...]
    unnamed x3 -> x0, blocking collectives: 17 us -> none
  transfers between devices with their start and end apart: 3 -> 0, of which waited for: 2 -> 0; matrix products, arithmetic and copies ran while one was open for 2% -> 0% of each run, Pallas kernels for 0% -> 0%
where the time goes in v1:
time: 109 us; the launch traced here: 108 us
  Pallas kernels  102 us (94%)
  local copies, waits for them, and re-layouts  5.17 us (5%)
  between operations  1.3 us (1%)
    pallas_call x1, Pallas kernels, local(): pl.pallas_call(functools.partial(kernel, R, C), out_shape=(jax.ShapeDtype...  102 us
    unnamed x8, local copies, waits for them, and re-layouts  5.17 us

profile of v1, /device:TPU:0, one launch (start us, length us, event | category | flops | bytes accessed | tf_op | source)
XLA Modules:
  0.0 108.5 jit_solution(5031920018326768266)
XLA Ops:
  1.3 1.6 %copy.8.pts = f32[256,64]{1,0:T(8,128)} copy(f32[256,64]{0,1:T(8,128)} %param.5) | data formatting | bytes 131072 | tf_op args[0]
  2.9 102.0 %shard_map.76 = (f32[1,256]{1,0:T(1,128)}, f32[1,256]{1,0:T(1,128)}, f32[256,256]{1,0:T(8,128)}) custom-call(f32[256,64]{1,0:T(8,128)} %copy.8.pts, f32[1,64]{1,0:T(1,128)} %bitcast.9, bf16[256,256]{1,0:T(8,128)(2,1)} %test.1, f32[1,256]{1,0:T(1,128)} %bitcast.6, f32[1,1]{1,0:T(1,128)} %bitcast.5.ridge), custom_call_target="tpu_custom_call" | custom-call | tf_op jit(solution)/shard_map/pallas_call | solution.py:388
  104.9 0.0 copy-start.1
  104.9 0.7 copy-done.1
  105.6 0.0 copy-start
  105.6 0.6 copy.13
  106.1 0.1 copy-done
  106.2 0.6 copy.14
  106.8 1.7 %copy.15 = f32[256,256]{1,0:T(8,128)} copy(f32[256,256]{1,0:T(8,128)} %get-tuple-element.14) | data formatting | bytes 524288
Async XLA Ops:
  104.9 0.7 copy-start.1
  105.6 0.7 copy-start

commit v2 on v1

--- a/solution.py
+++ b/solution.py
@@ -36,18 +36,24 @@
         ]
         rows = [a[k + i : k + i + 1, :] for i in range(width)]
         cols = [a[:, k + i : k + i + 1] for i in range(width)]
-        for t in range(width):
-            inverse = 1.0 / entry[t][t]
-            here = lane_row == k + t
-            rows[t] = jnp.where(here, inverse, rows[t] * inverse)
-            for j in range(t + 1, width):
-                entry[t][j] = entry[t][j] * inverse
+        for t in range(0, width, 2):
+            p, q, s, u = entry[t][t], entry[t][t + 1], entry[t + 1][t], entry[t + 1][t + 1]
+            inverse = 1.0 / (p * u - q * s)
+            p, q, s, u = u * inverse, -q * inverse, -s * inverse, p * inverse
+            here, next_one = lane_row == k + t, lane_row == k + t + 1
+            pair = here | next_one
+            one, two = rows[t], rows[t + 1]
+            rows[t] = jnp.where(here, p, jnp.where(next_one, q, p * one + q * two))
+            rows[t + 1] = jnp.where(here, s, jnp.where(next_one, u, s * one + u * two))
+            for j in range(t + 2, width):
+                one, two = entry[t][j], entry[t + 1][j]
+                entry[t][j], entry[t + 1][j] = p * one + q * two, s * one + u * two
             for i in range(width):
-                if i != t:
-                    factor = entry[i][t]
-                    rows[i] = jnp.where(here, 0.0, rows[i]) - factor * rows[t]
-                    for j in range(t + 1, width):
-                        entry[i][j] = entry[i][j] - factor * entry[t][j]
+                if i not in (t, t + 1):
+                    one, two = entry[i][t], entry[i][t + 1]
+                    rows[i] = jnp.where(pair, 0.0, rows[i]) - one * rows[t] - two * rows[t + 1]
+                    for j in range(t + 2, width):
+                        entry[i][j] = entry[i][j] - one * entry[t][j] - two * entry[t + 1][j]
         out = jnp.where((lane >= k) & (lane < k + width), 0.0, a)
         for t in range(width):
             out = out - cols[t] * rows[t]
@@ -65,11 +71,11 @@
 
 def kernel(
     R, C, pts, scale, test, tgt, ridge, coef_out, resid_out, sketch_out,
-    xrow, trow, xcol, left, left_norm, kmat, part, pair, srecv, core, crecv, crow, cgath, call, inv,
+    xrow, trow, xcol, left, left_norm, kmat, part, pair, srecv, core, crecv, crow, cgath, call, inv, spread_ref,
     vrow, vcol, qpart, qcol, send, recv, gather_send, gather_recv,
 ):
     r, c = lax.axis_index("row"), lax.axis_index("col")
-    n, feats = pts.shape
+    feats, n = pts.shape
     rank = test.shape[1]
     chunk = rank // C
     piece = chunk // R
@@ -121,12 +127,13 @@
     for i in range(1, C):
         pl.semaphore_signal(barrier, inc=1, device_id=to_col(i), device_id_type=MESH)
 
-    scaled = pts[...] * scale[...]
+    scaled = pts[...].T * scale[...]
     high = scaled.astype(jnp.bfloat16).astype(jnp.float32)
     both = jnp.concatenate([high, scaled - high], axis=1).astype(jnp.bfloat16)
     xrow[r] = both
     xcol[c] = both
     trow[r] = test[...]
+    part[...] = jnp.zeros_like(part)
     pl.semaphore_wait(barrier, R + C - 2)
     spread_col(xcol, X_COL)
 
@@ -167,23 +174,20 @@
         swapped = pltpu.roll(x, feats, 1)
         return swapped, x * (x + swapped)
 
-    def consume(slot, first=False):
+    def consume(slot):
         y = xrow[slot]
         right_norm = -0.5 * exact(ones, pair_sum(y.astype(jnp.float32))[1], NT)[0:1, :]
-        right = jnp.concatenate([y, y], axis=1)
-
-        def block(m, carry):
-            cross = lax.dot_general(left[m], right, NT, preferred_element_type=jnp.float32)
-            norm = left_norm[m]
-            weights = jnp.exp(cross + jnp.concatenate([norm] * (n // 128), axis=1) + right_norm)
-            kmat[slot, m] = weights
-            term = lax.dot_general(
-                weights.astype(jnp.bfloat16), trow[slot], NN, preferred_element_type=jnp.float32
-            )
-            part[m] = term if first else part[m] + term
-            return carry
-
-        lax.fori_loop(0, C, block, 0)
+        cross = lax.dot_general(
+            left[...].reshape(C * n, 4 * feats), jnp.concatenate([y, y], axis=1), NT,
+            preferred_element_type=jnp.float32,
+        )
+        norm = left_norm[...].reshape(C * n, 128)
+        weights = jnp.exp(cross + jnp.concatenate([norm] * (n // 128), axis=1) + right_norm)
+        kmat[slot] = weights.reshape(C, n, n)
+        term = lax.dot_general(
+            weights.astype(jnp.bfloat16), trow[slot], NN, preferred_element_type=jnp.float32
+        )
+        part[...] = part[...] + term.reshape(C, n, rank)
 
     def line(d):
         return ((along >= d, r - d * B), (along + d < A, r + d * B))
@@ -196,33 +200,29 @@
         swapped, square = pair_sum(x.astype(jnp.float32))
         left[m] = jnp.concatenate([x, swapped.astype(jnp.bfloat16)], axis=1)
         left_norm[m] = jnp.broadcast_to(-0.5 * jnp.sum(square, axis=1, keepdims=True), (n, 128))
-    consume(r, first=True)
-    for d in range(1, A):
-        for s in range(2):
-            for there, slot in line(d):
-
-                @pl.when(there)
-                def _(slot=slot, s=s):
+
+    def visit(t, carry):
+        turn, place = lax.div(t, 2 * A - 1), lax.rem(t, 2 * A - 1)
+        position = along + lax.div(place + 1, 2) * (1 - 2 * lax.rem(place, 2))
+
+        @pl.when((position >= 0) & (position < A))
+        def _():
+            slot = position * B + lax.rem(across + turn, B)
+            for s in range(2):
+
+                @pl.when(t > 0)
+                def _(s=s):
                     landed(slot, s)
+
+                @pl.when((t > 0) & (turn == 0))
+                def _(s=s):
                     forward(slot, s)
 
-        for there, slot in line(d):
-            pl.when(there)(functools.partial(consume, slot))
-    for i in range(1, B):
-        other = along * B + lax.rem(across + i, B)
-        for d in range(A):
-            for there, slot in line(d) if d else ((None, r),):
-                slot = slot - r + other
-
-                def use(slot=slot):
-                    landed(slot, 0)
-                    landed(slot, 1)
-                    consume(slot)
-
-                if there is None:
-                    use()
-                else:
-                    pl.when(there)(use)
+            consume(slot)
+
+        return carry
+
+    lax.fori_loop(0, B * (2 * A - 1), visit, 0)
 
     chip, side = lax.div(c, CORES), lax.rem(c, CORES)
     chips = C // CORES
@@ -287,6 +287,8 @@
     inv[half:, :half] = -corner
     inv[half:, half:] = second
 
+    spread_ref[...] = exact(inv[...], sketch, NT)
+
     def lanes(x):
         return jnp.sum(x, axis=1, keepdims=True)
 
@@ -294,8 +296,7 @@
         return jnp.broadcast_to(x[0:1, :], (1, 128))
 
     def precondition(resid, w):
-        solved = exact(jnp.broadcast_to(w, (8, rank)), inv[...], NN)
-        return (resid - exact(solved, sketch_out[...], NT)) / lam
+        return (resid - exact(jnp.broadcast_to(w, (8, rank)), spread_ref[...], NN)) / lam
 
     def operate(vector, inner, k):
         vec, sums = vrow.at[1 + 2 * k], qcol.at[k]
@@ -410,6 +411,7 @@
             pltpu.VMEM((R, rank // C // R, rank), f32),
             pltpu.VMEM((C, rank // C, rank), f32),
             pltpu.VMEM((rank, rank), f32),
+            pltpu.VMEM((rank, n), f32),
             pltpu.VMEM((5, R, 1, n + 128), f32),
             pltpu.VMEM((3, C, 1, n + 128), f32),
             pltpu.VMEM((2, C, 1, n + 128), f32),
@@ -422,7 +424,7 @@
         compiler_params=pltpu.CompilerParams(
             collective_id=0, has_side_effects=True, vmem_limit_bytes=56 * 1024 * 1024
         ),
-    )(points, feature_scale.reshape(1, feats), test_matrix, targets.reshape(1, n), ridge.reshape(1, 1))
+    )(points.T, feature_scale.reshape(1, feats), test_matrix, targets.reshape(1, n), ridge.reshape(1, 1))
     return coef.reshape(n), resid.reshape(n), sketch
 
 

time: 109 us -> 101 us (0.927)
  Pallas kernels: 102 us -> 96.3 us
  local copies, waits for them, and re-layouts: 5.17 us -> 3.57 us
    pallas_call x1, Pallas kernels: 102 us -> 96.3 us  [local(): pl.pallas_call(functools.partial(kernel, R, C), out_shape=(jax.ShapeDtype...]
    unnamed x8 -> x7, local copies, waits for them, and re-layouts: 5.17 us -> 3.57 us
where the time goes in v2:
time: 101 us
  Pallas kernels  96.3 us (95%)
  local copies, waits for them, and re-layouts  3.57 us (4%)
  between operations  1.3 us (1%)
    pallas_call x1, Pallas kernels, local(): pl.pallas_call(functools.partial(kernel, R, C), out_shape=(jax.ShapeDtype...  96.3 us
    unnamed x7, local copies, waits for them, and re-layouts  3.57 us

profile of v2, /device:TPU:0, one launch (start us, length us, event | category | flops | bytes accessed | tf_op | source)
XLA Modules:
  0.0 101.2 jit_solution(15848964640053976102)
XLA Ops:
  1.3 96.3 %shard_map.76 = (f32[1,256]{1,0:T(1,128)}, f32[1,256]{1,0:T(1,128)}, f32[256,256]{1,0:T(8,128)}) custom-call(f32[64,256]{1,0:T(8,128)} %bitcast.7, f32[1,64]{1,0:T(1,128)} %bitcast.11, bf16[256,256]{1,0:T(8,128)(2,1)} %test.1, f32[1,256]{1,0:T(1,128)} %bitcast.8, f32[1,1]{1,0:T(1,128)} %bitcast.6.ridge), custom_call_target="tpu_custom_call" | custom-call | tf_op jit(solution)/shard_map/pallas_call | solution.py:389
  97.6 0.0 copy-start.1
  97.6 0.7 copy-done.1
  98.3 0.0 copy-start
  98.3 0.6 copy.12
  98.9 0.1 copy-done
  99.0 0.6 copy.13
  99.5 1.7 %copy.14 = f32[256,256]{1,0:T(8,128)} copy(f32[256,256]{1,0:T(8,128)} %get-tuple-element.14) | data formatting | bytes 524288
Async XLA Ops:
  97.6 0.7 copy-start.1
  98.3 0.7 copy-start

commit v3 on v2

--- a/solution.py
+++ b/solution.py
@@ -12,9 +12,9 @@
 NN = (((1,), (0,)), ((), ()))
 NT = (((1,), (1,)), ((), ()))
 TN = (((0,), (0,)), ((), ()))
-X_COL, PAIR, SKETCH, CORE, CORE_ROW, CORE_ALL, CORE_COL, W_ROW, W_COL = range(9)
-Z_ROW, Q_COL, A_ROW, A_COL = (9, 13), (10, 14), (11, 15), (12, 16)
-ROUNDS = 17
+X_COL, PAIR, SKETCH, CORE, CORE_ROW, CORE_ALL, CORE_COL, W_ROW, W_COL, S_ALL = range(10)
+Z_ROW, Z_COL, Q_COL, FLAT = (10, 14), (11, 15), (12, 16), (13, 17)
+ROUNDS = 18
 CORES = 2
 
 
@@ -25,7 +25,7 @@
 
 
 def invert(a):
-    size, width = a.shape[0], 4
+    size, width = a.shape[0], 8
     lane = lax.broadcasted_iota(jnp.int32, a.shape, 1)
     lane_row = lane[0:1, :]
 
@@ -60,19 +60,18 @@
         return out, rows
 
     def turn(_, a):
-        a, upper = pivots(a, 0)
-        a = jnp.concatenate(upper + [a[width:, :]], axis=0)
-        a, lower = pivots(a, width)
-        a = jnp.concatenate([a[8:, :], a[:width, :]] + lower, axis=0)
-        return pltpu.roll(a, size - 8, 1)
-
-    return lax.fori_loop(0, size // 8, turn, a)
+        a, rows = pivots(a, 0)
+        a = jnp.concatenate([a[width:, :]] + rows, axis=0)
+        return pltpu.roll(a, size - width, 1)
+
+    return lax.fori_loop(0, size // width, turn, a)
 
 
 def kernel(
     R, C, pts, scale, test, tgt, ridge, coef_out, resid_out, sketch_out,
     xrow, trow, xcol, left, left_norm, kmat, part, pair, srecv, core, crecv, crow, cgath, call, inv, spread_ref,
-    vrow, vcol, qpart, qcol, send, recv, gather_send, gather_recv,
+    vrow, vcol, zrow, zcol, qpart, qcol, flat, flat_late, srow, send, recv, gather_send, gather_recv,
+    pair_send, pair_recv,
 ):
     r, c = lax.axis_index("row"), lax.axis_index("col")
     feats, n = pts.shape
@@ -107,6 +106,20 @@
         for i in range(1, C):
             push(buf.at[c], buf.at[c], k, to_col(i))
 
+    everyone = R * C
+    me = c * R + r
+
+    def device(i):
+        peer = lax.rem(me + i, everyone)
+        return (lax.rem(peer, R), lax.div(peer, R))
+
+    def spread_flat(buf, k):
+        def one(i, carry):
+            push(buf.at[me], buf.at[me], k, device(i))
+            return carry
+
+        lax.fori_loop(1, everyone, one, 0)
+
     def arrived(buf, k):
         part_of = buf.at[pl.ds(0, buf.shape[0] - 1)]
         pltpu.make_async_copy(part_of, part_of, recv.at[k]).wait()
@@ -122,10 +135,12 @@
         return acc
 
     barrier = pltpu.get_barrier_semaphore()
-    for i in range(1, R):
-        pl.semaphore_signal(barrier, inc=1, device_id=to_row(i), device_id_type=MESH)
-    for i in range(1, C):
-        pl.semaphore_signal(barrier, inc=1, device_id=to_col(i), device_id_type=MESH)
+
+    def greet(i, carry):
+        pl.semaphore_signal(barrier, inc=1, device_id=device(i), device_id_type=MESH)
+        return carry
+
+    lax.fori_loop(1, everyone, greet, 0)
 
     scaled = pts[...].T * scale[...]
     high = scaled.astype(jnp.bfloat16).astype(jnp.float32)
@@ -134,7 +149,7 @@
     xcol[c] = both
     trow[r] = test[...]
     part[...] = jnp.zeros_like(part)
-    pl.semaphore_wait(barrier, R + C - 2)
+    pl.semaphore_wait(barrier, everyone - 1)
     spread_col(xcol, X_COL)
 
     along, across = lax.div(r, B), lax.rem(r, B)
@@ -189,9 +204,6 @@
         )
         part[...] = part[...] + term.reshape(C, n, rank)
 
-    def line(d):
-        return ((along >= d, r - d * B), (along + d < A, r + d * B))
-
     for s in range(2):
         forward(r, s)
     arrived(xcol, X_COL)
@@ -201,38 +213,54 @@
         left[m] = jnp.concatenate([x, swapped.astype(jnp.bfloat16)], axis=1)
         left_norm[m] = jnp.broadcast_to(-0.5 * jnp.sum(square, axis=1, keepdims=True), (n, 128))
 
-    def visit(t, carry):
-        turn, place = lax.div(t, 2 * A - 1), lax.rem(t, 2 * A - 1)
-        position = along + lax.div(place + 1, 2) * (1 - 2 * lax.rem(place, 2))
-
-        @pl.when((position >= 0) & (position < A))
-        def _():
-            slot = position * B + lax.rem(across + turn, B)
-            for s in range(2):
-
-                @pl.when(t > 0)
-                def _(s=s):
-                    landed(slot, s)
-
-                @pl.when((t > 0) & (turn == 0))
-                def _(s=s):
-                    forward(slot, s)
-
-            consume(slot)
-
+    consume(r)
+
+    def sides(distance, action, line_of):
+        def one(side, carry):
+            position = along + distance * (2 * side - 1)
+
+            @pl.when((position >= 0) & (position < A) & ((distance > 0) | (side > 0)))
+            def _():
+                action(position * B + line_of)
+
+            return carry
+
+        lax.fori_loop(0, 2, one, 0)
+
+    def receive(slot):
+        for s in range(2):
+            landed(slot, s)
+            forward(slot, s)
+
+    def crossed(slot):
+        for s in range(2):
+            landed(slot, s)
+        consume(slot)
+
+    def level(d, carry):
+        sides(d, receive, across)
+        sides(d, consume, across)
+
+        def other(i, inner):
+            sides(d - 1, crossed, lax.rem(across + i, B))
+            return inner
+
+        lax.fori_loop(1, B, other, 0)
         return carry
 
-    lax.fori_loop(0, B * (2 * A - 1), visit, 0)
+    lax.fori_loop(1, A + 1, level, 0)
 
     chip, side = lax.div(c, CORES), lax.rem(c, CORES)
     chips = C // CORES
     for i in range(chips):
         m = lax.rem(chip + 1 + i, chips) * CORES + 1 - side
-        push(part.at[m], pair.at[m - 1 + side], PAIR, (r, chip * CORES + 1 - side))
-    mine = pair.at[pl.ds(0, chips)]
-    pltpu.make_async_copy(mine, mine, recv.at[PAIR]).wait()
+        copy(
+            part.at[m], pair.at[m - 1 + side], pair_send.at[i], pair_recv.at[i],
+            (r, chip * CORES + 1 - side),
+        ).start()
     for i in range(chips):
         m = lax.rem(chip + 1 + i, chips)
+        pltpu.make_async_copy(pair.at[0], pair.at[0], pair_recv.at[i]).wait()
         summed = part[m * CORES + side] + pair[m * CORES]
         if i < chips - 1:
             part[m * CORES + side] = summed
@@ -249,9 +277,8 @@
         core[i] = local[i * chunk : (i + 1) * chunk, :]
     for i in range(1, C):
         push(core.at[lax.rem(c + i, C)], crecv.at[c], CORE, to_col(i))
-    w_row, w_col = vrow.at[0], vcol.at[0]
-    w_row[r, :, 0:rank] = exact(resid, sketch, NN)[0:1, :]
-    w_row[r, :, rank : rank + 128] = jnp.zeros((1, 128), jnp.float32)
+    w_row, w_col = vrow, vcol
+    w_row[r] = exact(resid, sketch, NN)[0:1, :]
     spread_row(w_row, W_ROW)
     crecv[c] = core[c]
     arrived(crecv, CORE)
@@ -270,8 +297,10 @@
     arrived(cgath, CORE_ALL)
     call[c] = cgath[...].reshape(chunk, rank)
     spread_col(call, CORE_COL)
+    srow[c] = sketch
+    spread_col(srow, S_ALL)
     arrived(w_col, W_COL)
-    w = total(w_col)[:, 0:rank]
+    w = total(w_col)
     arrived(call, CORE_COL)
 
     whole = call[...].reshape(rank, rank)
@@ -292,69 +321,72 @@
     def lanes(x):
         return jnp.sum(x, axis=1, keepdims=True)
 
-    def wide(x):
-        return jnp.broadcast_to(x[0:1, :], (1, 128))
+    tag = lax.broadcasted_iota(jnp.int32, (1, 128), 1)
 
     def precondition(resid, w):
         return (resid - exact(jnp.broadcast_to(w, (8, rank)), spread_ref[...], NN)) / lam
 
-    def operate(vector, inner, k):
-        vec, sums = vrow.at[1 + 2 * k], qcol.at[k]
-        vec[r, :, 0:n] = vector[0:1, :]
-        vec[r, :, n : n + 128] = wide(lanes(inner))
-        spread_row(vec, Z_ROW[k])
-        arrived(vec, Z_ROW[k])
-        inner_sum = total(vec)[:, n : n + 128]
-        pieces = [vec[j] for j in range(R)]
-
-        def block(i, carry):
+    def operate(vector, extras, k):
+        first = k == 0
+        across, along, sums = zrow.at[k], zcol.at[k], qcol.at[k]
+        across[r] = vector[0:1, :]
+        along[c] = vector[0:1, :]
+        spread_row(across, Z_ROW[k])
+        spread_col(along, Z_COL[k])
+        own = lam * vector[0:1, :]
+        scalars = [lanes(own * vector[0:1, :])] + [lanes(x[0:1, :]) for x in extras]
+        if first:
+            projected = lam * exact(vector, sketch_out[...], NN)[0:1, :]
+            folded = jnp.zeros((8, rank), jnp.float32)
+            arrived(srow, S_ALL)
+        arrived(across, Z_ROW[k])
+        pieces = [across[j] for j in range(R)]
+        arrived(along, Z_COL[k])
+        for i in range(1, C + 1):
             m = lax.rem(c + i, C)
             acc = jnp.zeros((n, 128), jnp.float32)
             for j in range(R):
                 for h in range(0, n, 128):
                     acc += kmat[j, m, :, h : h + 128] * pieces[j][:, h : h + 128]
-            qpart[k, m, :, 0:n] = exact(ones, acc, NT)[0:1, :]
-            qpart[k, m, :, n : n + 128] = inner_sum
-
-            @pl.when(i < C)
-            def _():
+            row = exact(ones, acc, NT)[0:1, :]
+            if i < C:
+                qpart[k, m] = row
                 push(qpart.at[k, m], sums.at[c], Q_COL[k], (r, m))
-
-            return carry
-
-        lax.fori_loop(1, C + 1, block, 0)
-        sums[c] = qpart[k, c]
+            else:
+                sums[c] = row + own
+            scalars[0] += lanes(row * along[m])
+            if first:
+                folded += jnp.sum((lanes(acc) * srow[m]).reshape(n // 8, 8, rank), axis=0)
+        packed = jnp.zeros((1, 128), jnp.float32)
+        for i, x in enumerate(scalars):
+            packed = jnp.where(tag == i, x, packed)
+        shared = flat if first else flat_late
+        if first:
+            shared[me, :, 128 : 128 + rank] = projected + jnp.sum(folded, axis=0, keepdims=True)
+        shared[me, :, 0:128] = packed
+        spread_flat(shared, FLAT[k])
         arrived(sums, Q_COL[k])
-        out = total(sums)
-        return out[:, 0:n] + lam * vector, out[:, n : n + 1]
-
-    def reduce_all(row, scalar, k):
-        across, along = vrow.at[2 + 2 * k], vcol.at[1 + k]
-        across[r, :, 0:rank] = row[0:1, :]
-        across[r, :, rank : rank + 128] = wide(scalar)
-        spread_row(across, A_ROW[k])
-        arrived(across, A_ROW[k])
-        along[c] = total(across)
-        spread_col(along, A_COL[k])
-        arrived(along, A_COL[k])
-        out = total(along)
-        return out[:, 0:rank], out[:, rank : rank + 1]
+        image = total(sums)
+        arrived(shared, FLAT[k])
+        out = total(shared)
+        return image, [out[:, i : i + 1] for i in range(len(scalars))], out[:, 128:]
 
     direction = precondition(resid, w)
-    image, descent = operate(direction, resid * direction, 0)
-    projected, curve = reduce_all(exact(image, sketch_out[...], NN), lanes(direction * image), 0)
+    image, (curve, descent), projected = operate(direction, [resid * direction], 0)
     step = descent / curve
     coef = step * direction
     resid = resid - step * image
     precond = precondition(resid, w - step * projected)
-    next_image, fresh = operate(precond, resid * precond, 1)
+    late, (late_curve, fresh, mixed), _ = operate(precond, [resid * precond, precond * image], 1)
     ratio = fresh / descent
     direction = precond + ratio * direction
-    image = next_image + ratio * image
-    _, curve = reduce_all(direction, lanes(direction * image), 1)
-    step = fresh / curve
+    image = late + ratio * image
+    step = fresh / (late_curve + ratio * (2.0 * mixed + ratio * curve))
     coef_out[...] = (coef + step * direction)[0:1, :]
     resid_out[...] = (resid - step * image)[0:1, :]
+
+    def line(d):
+        return ((along >= d, r - d * B), (along + d < A, r + d * B))
 
     for s in range(2):
         for d in range(A):
@@ -366,7 +398,8 @@
                     else:
                         move.wait_send()
     sent(xcol, X_COL)
-    pltpu.make_async_copy(mine, mine, send.at[PAIR]).wait()
+    for i in range(chips):
+        pltpu.make_async_copy(pair.at[0], pair.at[0], pair_send.at[i]).wait()
     sent(srecv, SKETCH)
     sent(crecv, CORE)
     sent(crow.at[1], CORE_ROW)
@@ -374,11 +407,12 @@
     sent(call, CORE_COL)
     sent(w_row, W_ROW)
     sent(w_col, W_COL)
+    sent(srow, S_ALL)
     for k in range(2):
-        sent(vrow.at[1 + 2 * k], Z_ROW[k])
+        sent(zrow.at[k], Z_ROW[k])
+        sent(zcol.at[k], Z_COL[k])
         sent(qcol.at[k], Q_COL[k])
-        sent(vrow.at[2 + 2 * k], A_ROW[k])
-        sent(vcol.at[1 + k], A_COL[k])
+        sent((flat, flat_late)[k], FLAT[k])
 
 
 def local(R, C, points, feature_scale, test_matrix, targets, ridge):
@@ -412,14 +446,21 @@
             pltpu.VMEM((C, rank // C, rank), f32),
             pltpu.VMEM((rank, rank), f32),
             pltpu.VMEM((rank, n), f32),
-            pltpu.VMEM((5, R, 1, n + 128), f32),
-            pltpu.VMEM((3, C, 1, n + 128), f32),
-            pltpu.VMEM((2, C, 1, n + 128), f32),
-            pltpu.VMEM((2, C, 1, n + 128), f32),
+            pltpu.VMEM((R, 1, rank), f32),
+            pltpu.VMEM((C, 1, rank), f32),
+            pltpu.VMEM((2, R, 1, n), f32),
+            pltpu.VMEM((2, C, 1, n), f32),
+            pltpu.VMEM((2, C, 1, n), f32),
+            pltpu.VMEM((2, C, 1, n), f32),
+            pltpu.VMEM((R * C, 1, 128 + rank), f32),
+            pltpu.VMEM((R * C, 1, 128), f32),
+            pltpu.VMEM((C, n, rank), f32),
             pltpu.SemaphoreType.DMA((ROUNDS,)),
             pltpu.SemaphoreType.DMA((ROUNDS,)),
             pltpu.SemaphoreType.DMA((2, R, 6)),
             pltpu.SemaphoreType.DMA((2, R)),
+            pltpu.SemaphoreType.DMA((C,)),
+            pltpu.SemaphoreType.DMA((C,)),
         ],
         compiler_params=pltpu.CompilerParams(
             collective_id=0, has_side_effects=True, vmem_limit_bytes=56 * 1024 * 1024

time: 101 us -> 94.8 us (0.939)
  Pallas kernels: 96.3 us -> 89.7 us
    pallas_call x1, Pallas kernels: 96.3 us -> 89.7 us  [local(): pl.pallas_call(functools.partial(kernel, R, C), out_shape=(jax.ShapeDtype...]
where the time goes in v3:
time: 94.8 us; the launch traced here: 94.6 us
  Pallas kernels  89.7 us (95%)
  local copies, waits for them, and re-layouts  3.57 us (4%)
  between operations  1.3 us (1%)
    pallas_call x1, Pallas kernels, local(): pl.pallas_call(functools.partial(kernel, R, C), out_shape=(jax.ShapeDtype...  89.7 us
    unnamed x7, local copies, waits for them, and re-layouts  3.57 us

profile of v3, /device:TPU:0, one launch (start us, length us, event | category | flops | bytes accessed | tf_op | source)
XLA Modules:
  0.0 94.6 jit_solution(17461830074774585620)
XLA Ops:
  1.3 89.7 %shard_map.76 = (f32[1,256]{1,0:T(1,128)}, f32[1,256]{1,0:T(1,128)}, f32[256,256]{1,0:T(8,128)}) custom-call(f32[64,256]{1,0:T(8,128)} %bitcast.7, f32[1,64]{1,0:T(1,128)} %bitcast.11, bf16[256,256]{1,0:T(8,128)(2,1)} %test.1, f32[1,256]{1,0:T(1,128)} %bitcast.8, f32[1,1]{1,0:T(1,128)} %bitcast.6.ridge), custom_call_target="tpu_custom_call" | custom-call | tf_op jit(solution)/shard_map/pallas_call | solution.py:423
  91.0 0.0 copy-start.1
  91.0 0.7 copy-done.1
  91.7 0.0 copy-start
  91.7 0.6 copy.12
  92.3 0.1 copy-done
  92.4 0.6 copy.13
  92.9 1.7 %copy.14 = f32[256,256]{1,0:T(8,128)} copy(f32[256,256]{1,0:T(8,128)} %get-tuple-element.14) | data formatting | bytes 524288
Async XLA Ops:
  91.0 0.7 copy-start.1
  91.7 0.7 copy-start

commit v4 on v3

--- a/solution.py
+++ b/solution.py
@@ -16,6 +16,7 @@
 Z_ROW, Z_COL, Q_COL, FLAT = (10, 14), (11, 15), (12, 16), (13, 17)
 ROUNDS = 18
 CORES = 2
+BANDS = 4
 
 
 def exact(left, right, dims):
@@ -68,7 +69,7 @@
 
 
 def kernel(
-    R, C, pts, scale, test, tgt, ridge, coef_out, resid_out, sketch_out,
+    R, C, pts, scale, test, tgt, ridge, both_out, sketch_out,
     xrow, trow, xcol, left, left_norm, kmat, part, pair, srecv, core, crecv, crow, cgath, call, inv, spread_ref,
     vrow, vcol, zrow, zcol, qpart, qcol, flat, flat_late, srow, send, recv, gather_send, gather_recv,
     pair_send, pair_recv,
@@ -252,21 +253,28 @@
 
     chip, side = lax.div(c, CORES), lax.rem(c, CORES)
     chips = C // CORES
+    bands = [pl.ds(h * (n // BANDS), n // BANDS) for h in range(BANDS)]
     for i in range(chips):
         m = lax.rem(chip + 1 + i, chips) * CORES + 1 - side
-        copy(
-            part.at[m], pair.at[m - 1 + side], pair_send.at[i], pair_recv.at[i],
-            (r, chip * CORES + 1 - side),
-        ).start()
+        for h, band in enumerate(bands):
+            copy(
+                part.at[m, band], pair.at[m - 1 + side, band], pair_send.at[i, h], pair_recv.at[i, h],
+                (r, chip * CORES + 1 - side),
+            ).start()
     for i in range(chips):
         m = lax.rem(chip + 1 + i, chips)
-        pltpu.make_async_copy(pair.at[0], pair.at[0], pair_recv.at[i]).wait()
-        summed = part[m * CORES + side] + pair[m * CORES]
-        if i < chips - 1:
-            part[m * CORES + side] = summed
-            push(part.at[m * CORES + side], srecv.at[chip], SKETCH, (r, m * CORES + side))
-        else:
-            srecv[chip] = summed
+        for h, band in enumerate(bands):
+            here = pair.at[0, band]
+            pltpu.make_async_copy(here, here, pair_recv.at[i, h]).wait()
+            summed = part[m * CORES + side, band] + pair[m * CORES, band]
+            if i < chips - 1:
+                part[m * CORES + side, band] = summed
+                push(
+                    part.at[m * CORES + side, band], srecv.at[chip, band], SKETCH,
+                    (r, m * CORES + side),
+                )
+            else:
+                srecv[chip, band] = summed
     arrived(srecv, SKETCH)
     sketch = total(srecv)
     sketch_out[...] = sketch
@@ -316,7 +324,9 @@
     inv[half:, :half] = -corner
     inv[half:, half:] = second
 
-    spread_ref[...] = exact(inv[...], sketch, NT)
+    spread = exact(inv[...], sketch, NT)
+    left_over = sketch.T - exact(call[...].reshape(rank, rank), spread, NN)
+    spread_ref[...] = spread + exact(inv[...], left_over, NN)
 
     def lanes(x):
         return jnp.sum(x, axis=1, keepdims=True)
@@ -382,8 +392,8 @@
     direction = precond + ratio * direction
     image = late + ratio * image
     step = fresh / (late_curve + ratio * (2.0 * mixed + ratio * curve))
-    coef_out[...] = (coef + step * direction)[0:1, :]
-    resid_out[...] = (resid - step * image)[0:1, :]
+    both_out[:, 0:n] = (coef + step * direction)[0:1, :]
+    both_out[:, n : 2 * n] = (resid - step * image)[0:1, :]
 
     def line(d):
         return ((along >= d, r - d * B), (along + d < A, r + d * B))
@@ -399,7 +409,9 @@
                         move.wait_send()
     sent(xcol, X_COL)
     for i in range(chips):
-        pltpu.make_async_copy(pair.at[0], pair.at[0], pair_send.at[i]).wait()
+        for h, band in enumerate(bands):
+            here = pair.at[0, band]
+            pltpu.make_async_copy(here, here, pair_send.at[i, h]).wait()
     sent(srecv, SKETCH)
     sent(crecv, CORE)
     sent(crow.at[1], CORE_ROW)
@@ -420,15 +432,14 @@
     rank = test_matrix.shape[1]
     f32, half = jnp.float32, jnp.bfloat16
     vmem = pl.BlockSpec(memory_space=pltpu.VMEM)
-    coef, resid, sketch = pl.pallas_call(
+    both, sketch = pl.pallas_call(
         functools.partial(kernel, R, C),
         out_shape=(
-            jax.ShapeDtypeStruct((1, n), f32),
-            jax.ShapeDtypeStruct((1, n), f32),
+            jax.ShapeDtypeStruct((1, 2 * n), f32),
             jax.ShapeDtypeStruct((n, rank), f32),
         ),
         in_specs=[vmem, vmem, vmem, vmem, pl.BlockSpec(memory_space=pltpu.SMEM)],
-        out_specs=(vmem, vmem, vmem),
+        out_specs=(vmem, vmem),
         scratch_shapes=[
             pltpu.VMEM((R, n, 2 * feats), half),
             pltpu.VMEM((R, n, rank), half),
@@ -459,14 +470,14 @@
             pltpu.SemaphoreType.DMA((ROUNDS,)),
             pltpu.SemaphoreType.DMA((2, R, 6)),
             pltpu.SemaphoreType.DMA((2, R)),
-            pltpu.SemaphoreType.DMA((C,)),
-            pltpu.SemaphoreType.DMA((C,)),
+            pltpu.SemaphoreType.DMA((C, BANDS)),
+            pltpu.SemaphoreType.DMA((C, BANDS)),
         ],
         compiler_params=pltpu.CompilerParams(
             collective_id=0, has_side_effects=True, vmem_limit_bytes=56 * 1024 * 1024
         ),
     )(points.T, feature_scale.reshape(1, feats), test_matrix, targets.reshape(1, n), ridge.reshape(1, 1))
-    return coef.reshape(n), resid.reshape(n), sketch
+    return both[0, :n], both[0, n:], sketch
 
 
 def solution(mesh):

time: 94.8 us -> 95.2 us (level)
  Pallas kernels: 89.7 us -> 90.8 us
    unnamed x7 -> x3, local copies, waits for them, and re-layouts: 3.57 us -> 2.34 us
    pallas_call x1, Pallas kernels: 89.7 us -> 90.8 us  [local(): pl.pallas_call(functools.partial(kernel, R, C), out_shape=(jax.ShapeDtype...]
where the time goes in v4:
time: 95.2 us; the launch traced here: 95 us
  Pallas kernels  90.8 us (95%)
  local copies, waits for them, and re-layouts  2.91 us (3%)
  between operations  1.29 us (1%)
    pallas_call x1, Pallas kernels, local(): pl.pallas_call(functools.partial(kernel, R, C), out_shape=(jax.ShapeDtype...  90.8 us
    unnamed x3, local copies, waits for them, and re-layouts  2.34 us

profile of v4, /device:TPU:0, one launch (start us, length us, event | category | flops | bytes accessed | tf_op | source)
XLA Modules:
  0.0 95.0 jit_solution(16425315106948277000)
XLA Ops:
  1.3 90.8 %shard_map.76 = (f32[1,512]{1,0:T(1,128)}, f32[256,256]{1,0:T(8,128)}) custom-call(f32[64,256]{1,0:T(8,128)} %bitcast.7, f32[1,64]{1,0:T(1,128)} %bitcast.11, bf16[256,256]{1,0:T(8,128)(2,1)} %test.1, f32[1,256]{1,0:T(1,128)} %bitcast.8, f32[1,1]{1,0:T(1,128)} %bitcast.6.ridge), custom_call_target="tpu_custom_call" | custom-call | tf_op jit(solution)/shard_map/pallas_call | solution.py:435
  92.1 0.0 copy-start
  92.1 0.7 copy-done
  92.8 0.6 fusion
  93.4 1.7 %copy.10 = f32[256,256]{1,0:T(8,128)} copy(f32[256,256]{1,0:T(8,128)} %get-tuple-element.14) | data formatting | bytes 524288
Async XLA Ops:
  92.1 0.7 copy-start
